TPU v7x, 32 devices: a whole 2x2x4 slice. The times are simulated.
32 devices in a mesh: grp: 2 (over y), seq: 16 (over z, x, core).
Axes of the slice: x: 2, y: 2, z: 4, core: 2. Of those that a mesh axis runs over, the one named last changes fastest.
Arguments:
- queries: bfloat16 [8192, 1536], P(('grp', 'seq')), parts along dimension 0, may hold values from -6 to 6
- video_keys: bfloat16 [8192, 1536], P(('grp', 'seq')), parts along dimension 0, may hold values from -6 to 6
- video_values: bfloat16 [8192, 1536], P(('grp', 'seq')), parts along dimension 0, may hold values from -6 to 6
- attn_out: bfloat16 [8192, 1536], P(('grp', 'seq')), parts along dimension 0, may hold values from -1.796875 to 1.796875
- out_grad: bfloat16 [8192, 1536], P(('grp', 'seq')), parts along dimension 0, may hold values from -192 to 192
- log_sums: float32 [12, 8192], P(None, ('grp', 'seq')), parts along dimension 1, may hold values from 6.5 to 8
- text_keys: bfloat16 [512, 1536], P(('grp', 'seq')), parts along dimension 0, may hold values from -6 to 6
- text_values: bfloat16 [512, 1536], P(('grp', 'seq')), parts along dimension 0, may hold values from -6 to 6
- window: int32 [16, 3], replicated, may hold values from 0 to 1, as said below
- text_len: int32 [2], P('grp'), parts along dimension 0, may hold values from 64 to 256
Outputs:
- query_grad: bfloat16 [8192, 1536], P(('grp', 'seq')), parts along dimension 0
- key_grad: bfloat16 [8192, 1536], P(('grp', 'seq')), parts along dimension 0
- value_grad: bfloat16 [8192, 1536], P(('grp', 'seq')), parts along dimension 0
- textkey_grad: bfloat16 [512, 1536], P(('grp', 'seq')), parts along dimension 0
- textval_grad: bfloat16 [512, 1536], P(('grp', 'seq')), parts along dimension 0
There are 2 independent parts, one for each index of `grp`. A program takes and returns all parts, laid end to end along the dimension named above; an argument that names none is the same for every part. Nothing has to cross between parts.
Inputs may be any that keep to these rules, and one draw needn't show every extreme that they name: window[t, o] is 1 where query tile t attends video tile t + o - 1, else 0; the middle entry o = 1 is always 1, and entries naming a tile outside 0 .. 15 are 0. Text tokens at positions text_len[0] and beyond are padding.
All inputs are finite; a program needn't handle non-finite values.
Results may differ from a plain program's by a relative error of at most 0.0057.
Values may be sent and summed in bfloat16 or wider, within the bound.
A program may use at most 64 MiB of HBM per device.

v0:
```python
import jax
import jax.numpy as jnp
from jax import lax
from jax.sharding import PartitionSpec as P

HEADS = 12
HEAD_DIM = 128
TEXT = 256
REACH = 1


def shifted(value, axis, steps):
    count = lax.axis_size(axis)
    first, last = (max(0, -steps), min(count, count - steps))
    return lax.ppermute(value, axis, [(source, source + steps) for source in range(first, last)])


def rounded(value):
    return lax.optimization_barrier(value.astype(jnp.bfloat16)).astype(jnp.float32)


def block_grads(query_tile, grad_tile, sums_tile, deltas, key_tile, value_tile, column_w):
    factor = HEAD_DIM ** (-0.5)
    query_rows = query_tile.shape[0]
    key_rows = key_tile.shape[0]
    query_heads = query_tile.reshape(query_rows, HEADS, HEAD_DIM)
    grad_heads = grad_tile.reshape(query_rows, HEADS, HEAD_DIM)
    key_heads = key_tile.reshape(key_rows, HEADS, HEAD_DIM)
    value_heads = value_tile.reshape(key_rows, HEADS, HEAD_DIM)
    scores = (
        jnp.einsum("qhd,khd->hqk", query_heads, key_heads, preferred_element_type=jnp.float32)
        * factor
    )
    probs = jnp.exp(scores - sums_tile[:, :, None]) * column_w[None, None, :]
    dprobs = jnp.einsum("qhd,khd->hqk", grad_heads, value_heads, preferred_element_type=jnp.float32)
    dscores = (probs * (dprobs - deltas[:, :, None])).astype(jnp.bfloat16)
    probs_low = probs.astype(jnp.bfloat16)
    query_term = (
        jnp.einsum("hqk,khd->qhd", dscores, key_heads, preferred_element_type=jnp.float32).reshape(
            query_rows, HEADS * HEAD_DIM
        )
        * factor
    )
    key_term = (
        jnp.einsum(
            "hqk,qhd->khd", dscores, query_heads, preferred_element_type=jnp.float32
        ).reshape(key_rows, HEADS * HEAD_DIM)
        * factor
    )
    value_term = jnp.einsum(
        "hqk,qhd->khd", probs_low, grad_heads, preferred_element_type=jnp.float32
    ).reshape(key_rows, HEADS * HEAD_DIM)
    return (query_term, key_term, value_term)


def local(
    queries,
    video_keys,
    video_values,
    attn_out,
    out_grad,
    log_sums,
    text_keys,
    text_values,
    window,
    text_len,
):
    query_rows = queries.shape[0]
    features = queries.shape[1]
    here = lax.axis_index("seq")
    total = lax.axis_size("seq")
    deltas = jnp.sum(
        (out_grad.astype(jnp.float32) * attn_out.astype(jnp.float32)).reshape(
            query_rows, HEADS, HEAD_DIM
        ),
        axis=2,
    ).T
    every_tkey, every_tvalue = (
        lax.all_gather(text_keys, "seq", axis=0, tiled=True),
        lax.all_gather(text_values, "seq", axis=0, tiled=True),
    )
    text_valid = (jnp.arange(TEXT) < text_len[0]).astype(jnp.float32)
    text_q, text_k, caption_value_rows = block_grads(
        queries, out_grad, log_sums, deltas, every_tkey, every_tvalue, text_valid
    )
    query_gradient_running = rounded(text_q)
    key_gradient_running = jnp.zeros((query_rows, features), jnp.float32)
    value_gradient_running = jnp.zeros((query_rows, features), jnp.float32)
    own_row = lax.dynamic_slice_in_dim(window, here, 1, 0)[0].astype(jnp.float32)
    for offset in range(-REACH, REACH + 1):
        weight = jnp.full((query_rows,), own_row[offset + REACH], jnp.float32)
        if offset == 0:
            key_tile, value_tile = (video_keys, video_values)
        else:
            key_tile, value_tile = shifted((video_keys, video_values), "seq", -offset)
        grad_q, grad_k, grad_v = block_grads(
            queries, out_grad, log_sums, deltas, key_tile, value_tile, weight
        )
        query_gradient_running = query_gradient_running + rounded(grad_q)
        if offset == 0:
            key_gradient_running = key_gradient_running + rounded(grad_k)
            value_gradient_running = value_gradient_running + rounded(grad_v)
        else:
            back_keys, back_values = shifted(
                (grad_k.astype(jnp.bfloat16), grad_v.astype(jnp.bfloat16)), "seq", offset
            )
            key_gradient_running = key_gradient_running + back_keys.astype(jnp.float32)
            value_gradient_running = value_gradient_running + back_values.astype(jnp.float32)
    summed_k, summed_v = lax.psum((text_k, caption_value_rows), "seq")
    share = TEXT // total
    own_k = lax.dynamic_slice_in_dim(summed_k, here * share, share, 0)
    own_v = lax.dynamic_slice_in_dim(summed_v, here * share, share, 0)
    return (
        query_gradient_running.astype(jnp.bfloat16),
        key_gradient_running.astype(jnp.bfloat16),
        value_gradient_running.astype(jnp.bfloat16),
        own_k.astype(jnp.bfloat16),
        own_v.astype(jnp.bfloat16),
    )


def solution(mesh):
    return jax.shard_map(
        local,
        mesh=mesh,
        in_specs=(
            P(("grp", "seq"), None),
            P(("grp", "seq"), None),
            P(("grp", "seq"), None),
            P(("grp", "seq"), None),
            P(("grp", "seq"), None),
            P(None, ("grp", "seq")),
            P(("grp", "seq"), None),
            P(("grp", "seq"), None),
            P(),
            P("grp"),
        ),
        out_specs=(
            P(("grp", "seq"), None),
            P(("grp", "seq"), None),
            P(("grp", "seq"), None),
            P(("grp", "seq"), None),
            P(("grp", "seq"), None),
        ),
        check_vma=False,
    )
```

profile of v0, /device:TPU:1, one launch (start us, length us, event | category | flops | bytes accessed | tf_op | source)
XLA Modules:
  0.0 251.4 jit_solution(12690899248129534475)
XLA Ops:
  0.7 2.4 copy.103
  3.1 2.1 collective-permute-start.3
  5.2 4.5 %collective-permute-start.1 = (bf16[256,1536]{0,1:T(8,128)(2,1)}, bf16[256,1536]{0,1:T(8,128)(2,1)}, u32[]{:S(2)}, u32[]{:S(2)}) collective-permute-start(bf16[256,1536]{0,1:T(8,128)(2,1)} %copy.103), channel_id=1, source_target_pairs={{0,1},{1,2},{2,3},{3,4},{4,5},{5,6},{6,7},{7,8},{8,9},{9,10},{10,1... | collective-permute-start | bytes 2359304 | tf_op jit(solution)/shard_map/ppermute | solution.py:15
  9.6 1.2 copy.100
  10.8 1.9 collective-permute-start.2
  12.7 3.6 %collective-permute-start = (bf16[256,1536]{0,1:T(8,128)(2,1)}, bf16[256,1536]{0,1:T(8,128)(2,1)}, u32[]{:S(2)}, u32[]{:S(2)}) collective-permute-start(bf16[256,1536]{0,1:T(8,128)(2,1)} %copy.100), channel_id=1, source_target_pairs={{0,1},{1,2},{2,3},{3,4},{4,5},{5,6},{6,7},{7,8},{8,9},{9,10},{10,1... | collective-permute-start | bytes 2359304 | tf_op jit(solution)/shard_map/ppermute | solution.py:15
  17.0 0.3 copy.93
  17.3 0.0 copy-start.11
  17.3 0.0 copy-start.12
  17.3 0.3 copy.89
  17.6 0.8 copy-done.11
  18.5 1.2 copy.98
  19.6 38.6 %all_gather.6 = bf16[256,1536]{1,0:T(8,128)(2,1)S(1)} all-gather(bf16[16,1536]{1,0:T(8,128)(2,1)S(1)} %copy-done.12), channel_id=1, replica_groups=mesh['grp'=2,'seq'=16] {'seq'}, dimensions={0}, use_global_device_ids=true | all-gather | bytes 835584 | tf_op jit(solution)/shard_map/all_gather | solution.py:79
  58.2 0.3 copy.90
  58.5 23.4 %all_gather.7 = bf16[256,1536]{1,0:T(8,128)(2,1)S(1)} all-gather(bf16[16,1536]{1,0:T(8,128)(2,1)S(1)} %copy-done.13), channel_id=1, replica_groups=mesh['grp'=2,'seq'=16] {'seq'}, dimensions={0}, use_global_device_ids=true | all-gather | bytes 835584 | tf_op jit(solution)/shard_map/all_gather | solution.py:80
  81.9 1.1 copy.94
  83.0 2.5 convert_multiply_fusion
  85.5 1.5 reduce_sum.9
  87.0 0.6 fusion.38
  87.6 0.1 copy-done.7
  87.7 2.1 fusion.10
  89.8 1.6 multiply_convert_fusion.3
  91.3 1.5 multiply_convert_fusion.10
  92.9 1.5 convolution_multiply_fusion
  94.4 0.1 dynamic-slice_convert_fusion.2
  94.5 0.5 fusion.37
  95.0 1.6 copy.128
  96.6 3.1 %copy.127 = f32[256,1536]{1,0:T(8,128)} copy(f32[256,1536]{0,1:T(8,128)} %bitcast.109) | data formatting | bytes 3145728 | tf_op jit(solution)/shard_map/mul | solution.py:45
  99.8 1.2 copy.99
  101.0 1.7 fusion.40
  102.8 2.4 fusion.27
  105.2 3.2 %multiply_convert_fusion.1 = bf16[12,256,256]{2,1,0:T(8,128)(2,1)S(1)} fusion(f32[12,256,256]{2,1,0:T(8,128)S(1)} %fusion.40, bf16[256,12,128]{0,2,1:T(8,128)(2,1)S(1)} %bitcast.92, bf16[256,12,128]{0,2,1:T(8,128)(2,1)} %bitcast.16, f32[]{:T(128)} %bitcast.15, f32[12,256]{1,0:T(8,128)S(1)} %bitcast.122, f32[12,256]{1,0:T(8,128)S(1)} %copy-done.7), kind=kOutput, calls=%fused_computation.2 | convolution fusion | flops 206045184 | bytes 6316036 | tf_op jit(solution)/shard_map/qhd,khd->hqk/dot_general | solution.py:35
  108.5 2.3 copy.125
  110.8 77.0 %all-reduce.2 = (bf16[256,1536]{1,0:T(8,128)(2,1)}, bf16[256,1536]{1,0:T(8,128)(2,1)}) all-reduce(f32[256,1536]{1,0:T(8,128)} %copy.127, f32[256,1536]{1,0:T(8,128)} %copy.128), channel_id=1, replica_groups=mesh['grp'=2,'seq'=16] {'seq'}, use_global_device_ids=true, to_apply=%region_1.0 | all-reduce | flops 786432 | bytes 4718592 | tf_op jit(solution)/shard_map/psum | solution.py:109
  187.8 2.7 %multiply_convert_fusion.8 = bf16[12,256,128]{1,2,0:T(8,128)(2,1)} fusion(bf16[12,256,256]{2,1,0:T(8,128)(2,1)S(1)} %multiply_convert_fusion.1, bf16[256,12,128]{0,2,1:T(8,128)(2,1)} %bitcast.14), kind=kOutput, calls=%fused_computation.24 | convolution fusion | flops 202113024 | bytes 3145728 | tf_op jit(solution)/shard_map/hqk,khd->qhd/dot_general | solution.py:39
  190.4 2.3 copy.113
  192.7 1.3 multiply_convert_fusion.5
  194.0 2.3 copy.122
  196.3 1.5 dynamic-slice_convert_fusion
  197.8 1.7 fusion.39
  199.5 3.2 %multiply_convert_fusion.2 = bf16[12,256,256]{2,1,0:T(8,128)(2,1)S(1)} fusion(f32[12,256,256]{2,1,0:T(8,128)S(1)} %fusion.39, bf16[256,12,128]{0,2,1:T(8,128)(2,1)S(1)} %bitcast.93, bf16[256,12,128]{0,2,1:T(8,128)(2,1)} %bitcast.11, f32[]{:T(128)} %bitcast.10, f32[12,256]{1,0:T(8,128)S(1)} %bitcast.123, f32[12,256]{1,0:T(8,128)S(1)} %copy-done.7), kind=kOutput, calls=%fused_computation.4 | convolution fusion | flops 206045184 | bytes 6316036 | tf_op jit(solution)/shard_map/qhd,khd->hqk/dot_general | solution.py:35
  202.7 1.8 multiply_convert_fusion.9
  204.5 1.5 fusion.24
  206.1 1.3 multiply_convert_fusion.6
  207.3 1.2 copy.124
  208.5 2.3 copy.121
  210.8 1.2 copy.106
  212.0 1.9 collective-permute-start.4
  213.9 1.9 collective-permute-start.6
  215.8 1.7 fusion.41
  217.6 2.4 fusion.30
  220.0 3.2 %multiply_convert_fusion = bf16[12,256,256]{2,1,0:T(8,128)(2,1)S(1)} fusion(f32[12,256,256]{2,1,0:T(8,128)S(1)} %fusion.41, bf16[256,12,128]{0,2,1:T(8,128)(2,1)S(1)} %bitcast.96, bf16[256,12,128]{0,2,1:T(8,128)(2,1)} %bitcast.21, f32[]{:T(128)} %bitcast.20, f32[12,256]{1,0:T(8,128)S(1)} %bitcast.124, f32[12,256]{1,0:T(8,128)S(1)} %copy-done.7), kind=kOutput, calls=%fused_computation | convolution fusion | flops 206045184 | bytes 6316036 | tf_op jit(solution)/shard_map/qhd,khd->hqk/dot_general | solution.py:35
  223.1 2.3 copy.126
  225.4 0.4 multiply_convert_fusion.4
  225.8 1.2 copy.123
  227.0 3.6 %collective-permute-start.7 = (bf16[256,1536]{1,0:T(8,128)(2,1)}, bf16[256,1536]{1,0:T(8,128)(2,1)}, u32[]{:S(2)}, u32[]{:S(2)}) collective-permute-start(bf16[256,1536]{1,0:T(8,128)(2,1)} %copy.126), channel_id=1, source_target_pairs={{0,1},{1,2},{2,3},{3,4},{4,5},{5,6},{6,7},{7,8},{8,9},{9,10},{10,1... | collective-permute-start | bytes 2359304 | tf_op jit(solution)/shard_map/ppermute | solution.py:15
  230.6 1.8 multiply_convert_fusion.7
  232.4 0.3 copy.120
  232.7 2.5 %collective-permute-start.5 = (bf16[256,1536]{1,0:T(8,128)(2,1)}, bf16[256,1536]{1,0:T(8,128)(2,1)S(1)}, u32[]{:S(2)}, u32[]{:S(2)}) collective-permute-start(bf16[256,1536]{1,0:T(8,128)(2,1)} %copy.123), channel_id=1, source_target_pairs={{0,1},{1,2},{2,3},{3,4},{4,5},{5,6},{6,7},{7,8},{8,9},{9,10},{10,1... | collective-permute-start | bytes 2359304 | tf_op jit(solution)/shard_map/ppermute | solution.py:15
  235.3 2.4 add_convert_fusion.2
  237.7 3.0 %collective-permute-done.7 = bf16[256,1536]{1,0:T(8,128)(2,1)} collective-permute-done((bf16[256,1536]{1,0:T(8,128)(2,1)}, bf16[256,1536]{1,0:T(8,128)(2,1)}, u32[]{:S(2)}, u32[]{:S(2)}) %collective-permute-start.7) | collective-permute-done | bytes 786464 | tf_op jit(solution)/shard_map/ppermute | solution.py:15
  240.7 2.5 %add_convert_fusion = bf16[256,1536]{1,0:T(8,128)(2,1)} fusion(bf16[256,1536]{1,0:T(8,128)(2,1)} %collective-permute-done.7, bf16[256,1536]{1,0:T(8,128)(2,1)S(1)} %copy-done.1, bf16[256,1536]{1,0:T(8,128)(2,1)} %collective-permute-done.6), kind=kLoop, calls=%fused_computation.16 | loop fusion | flops 2359296 | bytes 3145728 | tf_op jit(solution)/shard_map/convert_element_type | solution.py:116
  243.2 5.9 %collective-permute-done.5 = bf16[256,1536]{1,0:T(8,128)(2,1)S(1)} collective-permute-done((bf16[256,1536]{1,0:T(8,128)(2,1)}, bf16[256,1536]{1,0:T(8,128)(2,1)S(1)}, u32[]{:S(2)}, u32[]{:S(2)}) %collective-permute-start.5) | collective-permute-done | bytes 786464 | tf_op jit(solution)/shard_map/ppermute | solution.py:15
  249.1 2.3 add_convert_fusion.1
  (33 shorter events, 0.1 us)
Async XLA Ops:
  0.6 9.0 %copy-start.8 = (bf16[256,1536]{1,0:T(8,128)(2,1)S(1)}, bf16[256,1536]{1,0:T(8,128)(2,1)}, u32[]{:S(2)}) copy-start(bf16[256,1536]{1,0:T(8,128)(2,1)} %param.11) | copy-start | bytes 2359300
  0.6 16.4 %copy-start.9 = (bf16[256,1536]{1,0:T(8,128)(2,1)S(1)}, bf16[256,1536]{1,0:T(8,128)(2,1)}, u32[]{:S(2)}) copy-start(bf16[256,1536]{1,0:T(8,128)(2,1)} %param.14) | copy-start | bytes 2359300
  3.1 14.3 %copy-start.10 = (bf16[256,1536]{1,0:T(8,128)(2,1)S(1)}, bf16[256,1536]{1,0:T(8,128)(2,1)}, u32[]{:S(2)}) copy-start(bf16[256,1536]{1,0:T(8,128)(2,1)} %param.10) | copy-start | bytes 2359300
  3.1 216.9 %collective-permute-start.3 = (bf16[256,1536]{0,1:T(8,128)(2,1)}, bf16[256,1536]{0,1:T(8,128)(2,1)}, u32[]{:S(2)}, u32[]{:S(2)}) collective-permute-start(bf16[256,1536]{0,1:T(8,128)(2,1)} %copy.103), channel_id=1, source_target_pairs={{1,0},{2,1},{3,2},{4,3},{5,4},{6,5},{7,6},{8,7},{9,8},{10,9},{11,1... | collective-permute-start | bytes 2359304 | tf_op jit(solution)/shard_map/ppermute | solution.py:15
  5.2 194.4 %collective-permute-start.1 = (bf16[256,1536]{0,1:T(8,128)(2,1)}, bf16[256,1536]{0,1:T(8,128)(2,1)}, u32[]{:S(2)}, u32[]{:S(2)}) collective-permute-start(bf16[256,1536]{0,1:T(8,128)(2,1)} %copy.103), channel_id=1, source_target_pairs={{0,1},{1,2},{2,3},{3,4},{4,5},{5,6},{6,7},{7,8},{8,9},{9,10},{10,1... | collective-permute-start | bytes 2359304 | tf_op jit(solution)/shard_map/ppermute | solution.py:15
  10.8 205.0 %collective-permute-start.2 = (bf16[256,1536]{0,1:T(8,128)(2,1)}, bf16[256,1536]{0,1:T(8,128)(2,1)}, u32[]{:S(2)}, u32[]{:S(2)}) collective-permute-start(bf16[256,1536]{0,1:T(8,128)(2,1)} %copy.100), channel_id=1, source_target_pairs={{1,0},{2,1},{3,2},{4,3},{5,4},{6,5},{7,6},{8,7},{9,8},{10,9},{11,1... | collective-permute-start | bytes 2359304 | tf_op jit(solution)/shard_map/ppermute | solution.py:15
  12.7 185.0 %collective-permute-start = (bf16[256,1536]{0,1:T(8,128)(2,1)}, bf16[256,1536]{0,1:T(8,128)(2,1)}, u32[]{:S(2)}, u32[]{:S(2)}) collective-permute-start(bf16[256,1536]{0,1:T(8,128)(2,1)} %copy.100), channel_id=1, source_target_pairs={{0,1},{1,2},{2,3},{3,4},{4,5},{5,6},{6,7},{7,8},{8,9},{9,10},{10,1... | collective-permute-start | bytes 2359304 | tf_op jit(solution)/shard_map/ppermute | solution.py:15
  17.3 1.1 copy-start.11
  17.3 2.3 copy-start.12
  19.6 38.9 %copy-start.13 = (bf16[16,1536]{1,0:T(8,128)(2,1)S(1)}, bf16[16,1536]{1,0:T(8,128)(2,1)}, u32[]{:S(2)}) copy-start(bf16[16,1536]{1,0:T(8,128)(2,1)} %param.17) | copy-start | bytes 147460
  87.0 0.7 copy-start.7
  87.7 2.1 copy-start.6
  92.9 1.6 copy-start.14
  92.9 2.2 copy-start
  96.6 3.1 %copy-start.3 = (bf16[12,256,128]{1,2,0:T(8,128)(2,1)S(1)}, bf16[12,256,128]{1,2,0:T(8,128)(2,1)}, u32[]{:S(2)}) copy-start(bf16[12,256,128]{1,2,0:T(8,128)(2,1)} %multiply_convert_fusion.10) | copy-start | bytes 2359300
  212.0 31.2 %collective-permute-start.4 = (bf16[256,1536]{1,0:T(8,128)(2,1)}, bf16[256,1536]{1,0:T(8,128)(2,1)}, u32[]{:S(2)}, u32[]{:S(2)}) collective-permute-start(bf16[256,1536]{1,0:T(8,128)(2,1)} %copy.121), channel_id=1, source_target_pairs={{1,0},{2,1},{3,2},{4,3},{5,4},{6,5},{7,6},{8,7},{9,8},{10,9},{11,1... | collective-permute-start | bytes 2359304 | tf_op jit(solution)/shard_map/ppermute | solution.py:15
  213.9 23.8 %collective-permute-start.6 = (bf16[256,1536]{1,0:T(8,128)(2,1)}, bf16[256,1536]{1,0:T(8,128)(2,1)}, u32[]{:S(2)}, u32[]{:S(2)}) collective-permute-start(bf16[256,1536]{1,0:T(8,128)(2,1)} %copy.124), channel_id=1, source_target_pairs={{1,0},{2,1},{3,2},{4,3},{5,4},{6,5},{7,6},{8,7},{9,8},{10,9},{11,1... | collective-permute-start | bytes 2359304 | tf_op jit(solution)/shard_map/ppermute | solution.py:15
  227.0 13.7 %collective-permute-start.7 = (bf16[256,1536]{1,0:T(8,128)(2,1)}, bf16[256,1536]{1,0:T(8,128)(2,1)}, u32[]{:S(2)}, u32[]{:S(2)}) collective-permute-start(bf16[256,1536]{1,0:T(8,128)(2,1)} %copy.126), channel_id=1, source_target_pairs={{0,1},{1,2},{2,3},{3,4},{4,5},{5,6},{6,7},{7,8},{8,9},{9,10},{10,1... | collective-permute-start | bytes 2359304 | tf_op jit(solution)/shard_map/ppermute | solution.py:15
  232.4 2.9 %copy-start.4 = (bf16[256,1536]{1,0:T(8,128)(2,1)S(1)}, bf16[256,1536]{1,0:T(8,128)(2,1)}, u32[]{:S(2)}) copy-start(bf16[256,1536]{1,0:T(8,128)(2,1)} %copy.99) | copy-start | bytes 2359300
  232.4 2.9 %copy-start.5 = (bf16[256,1536]{1,0:T(8,128)(2,1)S(1)}, bf16[256,1536]{1,0:T(8,128)(2,1)}, u32[]{:S(2)}) copy-start(bf16[256,1536]{1,0:T(8,128)(2,1)} %copy.113) | copy-start | bytes 2359300
  232.7 8.0 %copy-start.1 = (bf16[256,1536]{1,0:T(8,128)(2,1)S(1)}, bf16[256,1536]{1,0:T(8,128)(2,1)}, u32[]{:S(2)}) copy-start(bf16[256,1536]{1,0:T(8,128)(2,1)} %copy.125) | copy-start | bytes 2359300
  232.7 16.4 %collective-permute-start.5 = (bf16[256,1536]{1,0:T(8,128)(2,1)}, bf16[256,1536]{1,0:T(8,128)(2,1)S(1)}, u32[]{:S(2)}, u32[]{:S(2)}) collective-permute-start(bf16[256,1536]{1,0:T(8,128)(2,1)} %copy.123), channel_id=1, source_target_pairs={{0,1},{1,2},{2,3},{3,4},{4,5},{5,6},{6,7},{7,8},{8,9},{9,10},{10,1... | collective-permute-start | bytes 2359304 | tf_op jit(solution)/shard_map/ppermute | solution.py:15
  237.7 11.4 %copy-start.2 = (bf16[256,1536]{1,0:T(8,128)(2,1)S(1)}, bf16[256,1536]{1,0:T(8,128)(2,1)}, u32[]{:S(2)}) copy-start(bf16[256,1536]{1,0:T(8,128)(2,1)} %copy.122) | copy-start | bytes 2359300
where the time goes:
time: 254 us; the launch traced here: 251 us
  blocking collectives  139 us (55%)
  matrix products  37.7 us (15%)
  local copies, waits for them, and re-layouts  30.9 us (12%)
  starting transfers between devices  22.1 us (9%)
  other arithmetic  11.3 us (4%)
  waiting for transfers between devices  8.88 us (3%)
    psum x1, blocking collectives, local(): summed_k, summed_v = lax.psum((text_k, caption_value_rows), 'seq')  77 us
    all_gather x1, blocking collectives, local(): lax.all_gather(text_keys, 'seq', axis=0, tiled=True)  38.6 us
    all_gather x1, blocking collectives, local(): lax.all_gather(text_values, 'seq', axis=0, tiled=True)  23.4 us
    ppermute x8, starting transfers between devices, shifted(): lax.ppermute(value, axis, [(source, source + steps) for source in range(f...  22.1 us
    dot_general x4, matrix products, block_grads(): jnp.einsum('qhd,khd->hqk', grad_heads, value_heads, preferred_element_typ...  11.2 us
    optimization_barrier x6, local copies, waits for them, and re-layouts, rounded(): lax.optimization_barrier(value.astype(jnp.bfloat16)).astype(jnp.float32)  9.56 us
    ppermute x8, waiting for transfers between devices, shifted(): lax.ppermute(value, axis, [(source, source + steps) for source in range(f...  8.88 us
    dot_general x4, matrix products, block_grads(): jnp.einsum('hqk,qhd->khd', probs_low, grad_heads, preferred_element_type=...  8.42 us
  transfers between devices with their start and end apart: 8, of which 2 were waited for; matrix products, arithmetic and copies ran while one was open for 29% of the time, Pallas kernels for 0%

commit v1 on v0

v1 whole, which is shorter than its diff:
```python
import functools

import jax
import jax.numpy as jnp
from jax import lax
from jax.experimental import pallas as pl
from jax.experimental.pallas import tpu as pltpu
from jax.sharding import PartitionSpec as P

HEADS = 12
HEAD_DIM = 128
TEXT = 256
GROUP = 2
CHUNKS = HEADS // GROUP
FACTOR = HEAD_DIM ** (-0.5)
FAR = 1e30
MESH = pl.DeviceIdType.MESH


def mm(a, b, ca, cb):
    return lax.dot_general(a, b, (((ca,), (cb,)), ((), ())), preferred_element_type=jnp.float32)


def block_grads(q, g, k, v, sums, deltas, valid=None):
    probs = jnp.exp(mm(k, q, 1, 1) * FACTOR - sums)
    if valid is not None:
        probs = jnp.where(valid, probs, 0.0)
    dprobs = mm(v, g, 1, 1)
    dscores = (probs * (dprobs - deltas)).astype(jnp.bfloat16)
    dq = mm(dscores, k, 0, 0) * FACTOR
    dk = mm(dscores, q, 1, 0) * FACTOR
    dv = mm(probs.astype(jnp.bfloat16), g, 1, 0)
    return dq, dk, dv


def head(h):
    return pl.ds(pl.multiple_of(h * HEAD_DIM, HEAD_DIM), HEAD_DIM)


def kernel(
    n, inside, q_any, g_any, k_ref, v_ref, o_ref, sums_ref, tk_ref, tv_ref, win_ref, len_ref,
    dq_ref, dk_ref, dv_ref, tdk_ref, tdv_ref,
    q_ref, g_ref, nq, ng, stat, nstat, dq_sum, dk_sum, dv_sum, dq_out, dq_in, text, tgrad,
    local_sem, in_send, in_recv, stat_send, stat_recv, dq_send, dq_recv,
    *more,
):
    me = lax.axis_index("seq")
    has = (me > 0, me < n - 1)
    near = (me - 1, me + 1)
    share = TEXT // n
    half, outer = n // 2, n // 4
    core, cross_bit, layer = lax.rem(me, 2), lax.rem(me // 2, 2), me // 4
    mate, cross = me + 1 - 2 * core, me + 2 - 4 * cross_bit
    peers = [lax.rem(layer + d, outer) * 4 + lax.rem(me, 4) for d in range(1, outer)]

    loads = [
        pltpu.make_async_copy(q_any, q_ref, local_sem.at[0]),
        pltpu.make_async_copy(g_any, g_ref, local_sem.at[1]),
    ]
    for load in loads:
        load.start()

    def signal(device):
        pl.semaphore_signal(barrier, inc=1, device_id={"seq": device}, device_id_type=MESH)

    def remote(src, dst, send, recv, device):
        return pltpu.make_async_remote_copy(
            src_ref=src, dst_ref=dst, send_sem=send, recv_sem=recv,
            device_id={"seq": device}, device_id_type=MESH,
        )

    barrier = pltpu.get_barrier_semaphore()
    for side in range(2):
        pl.when(has[side])(functools.partial(signal, near[side]))
    far = [cross] + peers if inside else []
    for device in far:
        signal(device)
    pl.semaphore_wait(barrier, len(far) + sum(side.astype(jnp.int32) for side in has))

    def columns(c):
        return pl.ds(pl.multiple_of(c * GROUP * HEAD_DIM, GROUP * HEAD_DIM), GROUP * HEAD_DIM)

    def in_copies(side, c):
        there = 1 - side
        return [
            remote(
                src.at[:, columns(c)], dst.at[there, :, columns(c)],
                in_send.at[i, there, c], in_recv.at[i, there, c], near[side],
            )
            for i, (src, dst) in enumerate(((q_any, nq), (g_any, ng)))
        ]

    def stat_copy(side):
        there = 1 - side
        return remote(
            stat.at[side], nstat.at[there], stat_send.at[there], stat_recv.at[there], near[side]
        )

    def dq_copy(side, c):
        there = 1 - side
        return remote(
            dq_out.at[side, :, columns(c)], dq_in.at[there, :, columns(c)],
            dq_send.at[there, c], dq_recv.at[there, c], near[side],
        )

    if inside:
        t_send, t_recv, part1, got1, part2, got2, sum3, part3, got3, r1, r2, r3 = more

        def slot(device):
            return lax.rem(device, 2) * half + device // 2

        def rows(device):
            return pl.ds(pl.multiple_of(slot(device) * share, share), share)

        def text_copy(piece, device, index):
            ref = text.at[:, rows(piece), :]
            return remote(ref, ref, t_send.at[index], t_recv.at[piece], device)

        text[0, rows(me), :] = tk_ref[...]
        text[1, rows(me), :] = tv_ref[...]
        text_copies = []

        def push(piece, device):
            copy = text_copy(piece, device, len(text_copies))
            copy.start()
            text_copies.append(copy)

        push(me, cross)
        for peer in peers:
            push(me, peer)
        push(me, mate)

    for side in range(2):

        @pl.when(has[side])
        def _():
            def step(c, carry):
                for copy in in_copies(side, c):
                    copy.start()
                return carry

            lax.fori_loop(0, CHUNKS, step, 0)

    for load in loads:
        load.wait()

    def delta_step(h, carry):
        cols = head(h)
        prod = g_ref[:, cols].astype(jnp.float32) * o_ref[:, cols].astype(jnp.float32)
        row = jnp.sum(prod.T, axis=0, keepdims=True)
        for side in range(3):
            stat[side, pl.ds(HEADS + h, 1), :] = row
        return carry

    lax.fori_loop(0, HEADS, delta_step, 0)
    for index, offset in enumerate((0, 2, 1)):
        bias = jnp.where(win_ref[me, offset] > 0, 0.0, FAR).astype(jnp.float32)
        stat[index, :HEADS, :] = sums_ref[...] + bias
    for side in range(2):

        @pl.when(has[side])
        def _():
            stat_copy(side).start()

        @pl.when(jnp.logical_not(has[side]))
        def _():
            nq[side] = jnp.zeros(nq.shape[1:], nq.dtype)
            ng[side] = jnp.zeros(ng.shape[1:], ng.dtype)
            dq_in[side] = jnp.zeros(dq_in.shape[1:], dq_in.dtype)
            nstat[side] = jnp.full(nstat.shape[1:], FAR, nstat.dtype)

    if inside:
        text_copy(cross, cross, 0).wait_recv()
        for peer in peers:
            push(cross, peer)
        push(cross, mate)

    def own_step(h, carry):
        cols = head(h)
        dq, dk, dv = block_grads(
            q_ref[:, cols], g_ref[:, cols], k_ref[:, cols], v_ref[:, cols],
            stat[2, pl.ds(h, 1), :], stat[2, pl.ds(HEADS + h, 1), :],
        )
        dq_sum[:, cols] = dq
        dk_sum[:, cols] = dk
        dv_sum[:, cols] = dv
        return carry

    lax.fori_loop(0, HEADS, own_step, 0)

    line = lax.broadcasted_iota(jnp.int32, (TEXT, 1), 0)
    if inside:
        for peer in peers:
            for piece in (peer, peer + 2 - 4 * cross_bit):
                text_copy(piece, mate, 0).wait_recv()
                push(piece, mate)
        for device in [me] + peers:
            mates = device + 1 - 2 * core
            for piece in (mates, mates + 2 - 4 * cross_bit):
                text_copy(piece, mate, 0).wait_recv()
        spot = line // share
        place = (lax.rem(spot, half) * 2 + spot // half) * share + lax.rem(line, share)
    else:
        text[0] = tk_ref[...]
        text[1] = tv_ref[...]
        place = line
    valid = place < len_ref[0]

    def text_step(h, carry):
        cols = head(h)
        dq, dk, dv = block_grads(
            q_ref[:, cols], g_ref[:, cols], text[0, :, cols], text[1, :, cols],
            sums_ref[pl.ds(h, 1), :], stat[2, pl.ds(HEADS + h, 1), :], valid,
        )
        dq_sum[:, cols] += dq
        tgrad[0, :, cols] = dk
        tgrad[1, :, cols] = dv
        return carry

    lax.fori_loop(0, HEADS, text_step, 0)

    if inside:
        rest = half * share
        pair = 2 * share

        def span(start, size):
            return pl.ds(pl.multiple_of(start, share), size)

        part1[...] = tgrad[:, span((1 - core) * rest, rest), :].astype(jnp.bfloat16)
        copy1 = remote(part1, got1, r1.at[0], r1.at[1], mate)
        copy1.start()

    def window_step(c, carry):
        for side in range(2):

            @pl.when(has[side])
            def _():
                for copy in in_copies(1 - side, c):
                    copy.wait_recv()

        for i in range(GROUP):
            h = c * GROUP + i
            cols = head(h)
            dk_all, dv_all = dk_sum[:, cols], dv_sum[:, cols]
            for side in range(2):
                dq, dk, dv = block_grads(
                    nq[side, :, cols], ng[side, :, cols], k_ref[:, cols], v_ref[:, cols],
                    nstat[side, pl.ds(h, 1), :], nstat[side, pl.ds(HEADS + h, 1), :],
                )
                dq_out[side, :, cols] = dq.astype(jnp.bfloat16)
                dk_all, dv_all = dk_all + dk, dv_all + dv
            dk_ref[:, cols] = dk_all.astype(jnp.bfloat16)
            dv_ref[:, cols] = dv_all.astype(jnp.bfloat16)
        for side in range(2):

            @pl.when(has[side])
            def _():
                dq_copy(side, c).start()

        return carry

    for side in range(2):

        @pl.when(has[side])
        def _():
            stat_copy(1 - side).wait_recv()

    lax.fori_loop(0, CHUNKS // 3, window_step, 0)

    if inside:
        copy1.wait_recv()
        copies2 = []
        for d in range(1, outer):
            there = lax.rem(layer + d, outer)
            part2[d - 1] = (
                tgrad[:, span(core * rest + there * pair, pair), :]
                + got1[:, span(there * pair, pair), :].astype(jnp.float32)
            ).astype(jnp.bfloat16)
            copy = remote(
                part2.at[d - 1], got2.at[d - 1], r2.at[0, d - 1], r2.at[1, d - 1], peers[d - 1]
            )
            copy.start()
            copies2.append(copy)

    lax.fori_loop(CHUNKS // 3, CHUNKS - 1, window_step, 0)

    if inside:
        total = tgrad[:, span(core * rest + layer * pair, pair), :] + got1[
            :, span(layer * pair, pair), :
        ].astype(jnp.float32)
        for d, copy in enumerate(copies2):
            copy.wait_recv()
            total = total + got2[d].astype(jnp.float32)
        sum3[...] = total
        part3[...] = sum3[:, span((1 - cross_bit) * share, share), :].astype(jnp.bfloat16)
        copy3 = remote(part3, got3, r3.at[0], r3.at[1], cross)
        copy3.start()

    lax.fori_loop(CHUNKS - 1, CHUNKS, window_step, 0)

    if inside:
        copy3.wait_recv()
        mine = sum3[:, span(cross_bit * share, share), :] + got3[...].astype(jnp.float32)
        tdk_ref[...] = mine[0].astype(jnp.bfloat16)
        tdv_ref[...] = mine[1].astype(jnp.bfloat16)
    else:
        tdk_ref[...] = tgrad[0]
        tdv_ref[...] = tgrad[1]

    def last_step(c, carry):
        for side in range(2):

            @pl.when(has[side])
            def _():
                dq_copy(1 - side, c).wait_recv()

        cols = columns(c)
        dq_ref[:, cols] = (
            dq_sum[:, cols]
            + dq_in[0, :, cols].astype(jnp.float32)
            + dq_in[1, :, cols].astype(jnp.float32)
        ).astype(jnp.bfloat16)
        return carry

    lax.fori_loop(0, CHUNKS, last_step, 0)

    for side in range(2):

        @pl.when(has[side])
        def _():
            def step(c, carry):
                for copy in in_copies(side, c):
                    copy.wait_send()
                dq_copy(side, c).wait_send()
                return carry

            lax.fori_loop(0, CHUNKS, step, 0)
            stat_copy(side).wait_send()

    if inside:
        for copy in text_copies + [copy1] + copies2 + [copy3]:
            copy.wait_send()


def local(
    queries, video_keys, video_values, attn_out, out_grad, log_sums, text_keys, text_values,
    window, text_len,
):
    n = lax.axis_size("seq")
    tile, width = queries.shape
    share = TEXT // n
    inside = n % 4 == 0 and n >= 8 and share % 16 == 0
    low, wide = jnp.bfloat16, jnp.float32
    if not inside:
        text_keys = lax.all_gather(text_keys, "seq", axis=0, tiled=True)
        text_values = lax.all_gather(text_values, "seq", axis=0, tiled=True)
    text_out = jax.ShapeDtypeStruct(text_keys.shape, low if inside else wide)
    vmem, dma = pltpu.VMEM, pltpu.SemaphoreType.DMA
    scratch = [
        vmem((tile, width), low), vmem((tile, width), low),
        vmem((2, tile, width), low), vmem((2, tile, width), low),
        vmem((3, 2 * HEADS, tile), wide), vmem((2, 2 * HEADS, tile), wide),
        vmem((tile, width), wide), vmem((tile, width), wide), vmem((tile, width), wide),
        vmem((2, tile, width), low), vmem((2, tile, width), low),
        vmem((2, TEXT, width), low), vmem((2, TEXT, width), wide),
        dma((2,)), dma((2, 2, CHUNKS)), dma((2, 2, CHUNKS)),
        dma((2,)), dma((2,)), dma((2, CHUNKS)), dma((2, CHUNKS)),
    ]
    if inside:
        scratch += [
            dma((n - 1,)), dma((n,)),
            vmem((2, TEXT // 2, width), low), vmem((2, TEXT // 2, width), low),
            vmem((n // 4 - 1, 2, 2 * share, width), low), vmem((n // 4 - 1, 2, 2 * share, width), low),
            vmem((2, 2 * share, width), wide),
            vmem((2, share, width), low), vmem((2, share, width), low),
            dma((2,)), dma((2, n // 4 - 1)), dma((2,)),
        ]
    hbm, on_chip = pl.BlockSpec(memory_space=pl.ANY), pl.BlockSpec(memory_space=pltpu.VMEM)
    scalars = pl.BlockSpec(memory_space=pltpu.SMEM)
    video_out = jax.ShapeDtypeStruct((tile, width), low)
    dq, dk, dv, tdk, tdv = pl.pallas_call(
        functools.partial(kernel, n, inside),
        out_shape=(video_out, video_out, video_out, text_out, text_out),
        in_specs=[hbm, hbm] + [on_chip] * 6 + [scalars] * 2,
        out_specs=[on_chip] * 5,
        scratch_shapes=scratch,
        compiler_params=pltpu.CompilerParams(
            collective_id=0, has_side_effects=True, vmem_limit_bytes=48 * 2**20
        ),
    )(
        queries, out_grad, video_keys, video_values, attn_out, log_sums, text_keys, text_values,
        window, text_len,
    )
    if not inside:
        tdk = lax.psum_scatter(tdk, "seq", scatter_dimension=0, tiled=True).astype(low)
        tdv = lax.psum_scatter(tdv, "seq", scatter_dimension=0, tiled=True).astype(low)
    return dq, dk, dv, tdk, tdv


def solution(mesh):
    rows, every = P(("grp", "seq"), None), P()
    return jax.shard_map(
        local,
        mesh=mesh,
        in_specs=(rows, rows, rows, rows, rows, P(None, ("grp", "seq")), rows, rows, every, P("grp")),
        out_specs=(rows, rows, rows, rows, rows),
        check_vma=False,
    )
```

time: 254 us -> 88.7 us (0.35)
  the two profiles are of different devices: /device:TPU:1 before, /device:TPU:19 now
where the time goes in v1:
time: 88.7 us; the launch traced here: 88.1 us
  Pallas kernels  75.3 us (85%)
  local copies, waits for them, and re-layouts  11.5 us (13%)
  between operations  1.3 us (1%)
    pallas_call x1, Pallas kernels, local(): pl.pallas_call(functools.partial(kernel, n, inside), out_shape=(video_out...  75.3 us
    unnamed x20, local copies, waits for them, and re-layouts  11.5 us

profile of v1, /device:TPU:19, one launch (start us, length us, event | category | flops | bytes accessed | tf_op | source)
XLA Modules:
  0.0 88.1 jit_solution(17185335331623702335)
XLA Ops:
  1.3 0.8 copy.15.win_ref
  2.0 0.0 copy-start
  2.0 1.1 %copy-done = bf16[256,1536]{1,0:T(8,128)(2,1)S(1)} copy-done((bf16[256,1536]{1,0:T(8,128)(2,1)S(1)}, bf16[256,1536]{1,0:T(8,128)(2,1)}, u32[]{:S(2)}) %copy-start) | copy-done | bytes 786456
  3.2 0.0 copy-start.1
  3.2 1.1 %copy-done.1 = bf16[256,1536]{1,0:T(8,128)(2,1)S(1)} copy-done((bf16[256,1536]{1,0:T(8,128)(2,1)S(1)}, bf16[256,1536]{1,0:T(8,128)(2,1)}, u32[]{:S(2)}) %copy-start.1) | copy-done | bytes 786456
  4.3 0.0 copy-start.2
  4.3 1.1 %copy-done.2 = bf16[256,1536]{1,0:T(8,128)(2,1)S(1)} copy-done((bf16[256,1536]{1,0:T(8,128)(2,1)S(1)}, bf16[256,1536]{1,0:T(8,128)(2,1)}, u32[]{:S(2)}) %copy-start.2) | copy-done | bytes 786456
  5.4 0.0 copy-start.3
  5.4 1.1 %copy-done.3 = bf16[256,1536]{1,0:T(8,128)(2,1)S(1)} copy-done((bf16[256,1536]{1,0:T(8,128)(2,1)S(1)}, bf16[256,1536]{1,0:T(8,128)(2,1)}, u32[]{:S(2)}) %copy-start.3) | copy-done | bytes 786456
  6.6 0.0 copy-start.4
  6.6 0.8 copy-done.4
  7.4 0.0 copy-start.5
  7.4 0.8 copy-done.5
  8.2 0.0 copy-start.6
  8.2 0.7 copy-done.6
  8.9 75.3 %shard_map.137 = (bf16[256,1536]{1,0:T(8,128)(2,1)S(1)}, bf16[256,1536]{1,0:T(8,128)(2,1)S(1)}, bf16[256,1536]{1,0:T(8,128)(2,1)S(1)}, bf16[16,1536]{1,0:T(8,128)(2,1)S(1)}, bf16[16,1536]{1,0:T(8,128)(2,1)S(1)}) custom-call(bf16[256,1536]{1,0:T(8,128)(2,1)S(1)} %copy-done, bf16[256,1536]{1,0:T(8,128)(2,1)S(1)} %copy-done.1, bf16[256,1536]{1,0:T(8,128)(2,1)S(1)} %copy-done.2, ...), custom_call_target="tpu_custom_call" | custom-call | tf_op jit(solution)/shard_map/pallas_call | solution.py:381
  84.2 0.9 %copy.22 = bf16[256,1536]{1,0:T(8,128)(2,1)} copy(bf16[256,1536]{1,0:T(8,128)(2,1)S(1)} %get-tuple-element.10) | data formatting | bytes 1572864
  85.1 0.9 copy.23
  86.0 0.9 copy.24
  86.9 0.6 copy.25
  87.5 0.6 copy.26
Async XLA Ops:
  2.0 1.1 %copy-start = (bf16[256,1536]{1,0:T(8,128)(2,1)S(1)}, bf16[256,1536]{1,0:T(8,128)(2,1)}, u32[]{:S(2)}) copy-start(bf16[256,1536]{1,0:T(8,128)(2,1)} %q_any.1) | copy-start | bytes 2359300
  3.2 1.1 %copy-start.1 = (bf16[256,1536]{1,0:T(8,128)(2,1)S(1)}, bf16[256,1536]{1,0:T(8,128)(2,1)}, u32[]{:S(2)}) copy-start(bf16[256,1536]{1,0:T(8,128)(2,1)} %g_any.1) | copy-start | bytes 2359300
  4.3 1.1 %copy-start.2 = (bf16[256,1536]{1,0:T(8,128)(2,1)S(1)}, bf16[256,1536]{1,0:T(8,128)(2,1)}, u32[]{:S(2)}) copy-start(bf16[256,1536]{1,0:T(8,128)(2,1)} %k_ref.1) | copy-start | bytes 2359300
  5.4 1.1 %copy-start.3 = (bf16[256,1536]{1,0:T(8,128)(2,1)S(1)}, bf16[256,1536]{1,0:T(8,128)(2,1)}, u32[]{:S(2)}) copy-start(bf16[256,1536]{1,0:T(8,128)(2,1)} %v_ref.1) | copy-start | bytes 2359300
  6.6 0.8 copy-start.4
  7.4 0.8 copy-start.5
  8.2 0.7 copy-start.6

commit v2 on v1

--- a/solution.py
+++ b/solution.py
@@ -38,9 +38,9 @@
 
 
 def kernel(
-    n, inside, q_any, g_any, k_ref, v_ref, o_ref, sums_ref, tk_ref, tv_ref, win_ref, len_ref,
+    n, inside, q_any, g_any, k_any, v_any, o_any, sums_ref, tk_any, tv_any, win_ref, len_ref,
     dq_ref, dk_ref, dv_ref, tdk_ref, tdv_ref,
-    q_ref, g_ref, nq, ng, stat, nstat, dq_sum, dk_sum, dv_sum, dq_out, dq_in, text, tgrad,
+    q_ref, g_ref, k_ref, v_ref, o_ref, nq, ng, stat, nstat, dq_sum, dk_sum, dv_sum, dq_out, dq_in, text, tgrad,
     local_sem, in_send, in_recv, stat_send, stat_recv, dq_send, dq_recv,
     *more,
 ):
@@ -53,9 +53,14 @@
     mate, cross = me + 1 - 2 * core, me + 2 - 4 * cross_bit
     peers = [lax.rem(layer + d, outer) * 4 + lax.rem(me, 4) for d in range(1, outer)]
 
+    own_text = pl.ds(pl.multiple_of((core * half + me // 2) * share, share), share)
     loads = [
-        pltpu.make_async_copy(q_any, q_ref, local_sem.at[0]),
-        pltpu.make_async_copy(g_any, g_ref, local_sem.at[1]),
+        pltpu.make_async_copy(src, dst, local_sem.at[i])
+        for i, (src, dst) in enumerate((
+            (tk_any, text.at[0, own_text, :] if inside else text.at[0]),
+            (tv_any, text.at[1, own_text, :] if inside else text.at[1]),
+            (g_any, g_ref), (o_any, o_ref), (q_any, q_ref), (k_any, k_ref), (v_any, v_ref),
+        ))
     ]
     for load in loads:
         load.start()
@@ -112,23 +117,49 @@
         def rows(device):
             return pl.ds(pl.multiple_of(slot(device) * share, share), share)
 
-        def text_copy(piece, device, index):
+        def text_copy(piece, device, kind):
             ref = text.at[:, rows(piece), :]
-            return remote(ref, ref, t_send.at[index], t_recv.at[piece], device)
-
-        text[0, rows(me), :] = tk_ref[...]
-        text[1, rows(me), :] = tv_ref[...]
-        text_copies = []
-
-        def push(piece, device):
-            copy = text_copy(piece, device, len(text_copies))
-            copy.start()
-            text_copies.append(copy)
-
-        push(me, cross)
-        for peer in peers:
-            push(me, peer)
-        push(me, mate)
+            return remote(ref, ref, t_send.at[kind, piece], t_recv.at[piece], device)
+
+        def pair(at):
+            own = at * 4 + lax.rem(me, 4)
+            return own, own + 2 - 4 * cross_bit
+
+        pushed = []
+
+        def push(pieces, device, kind, condition=None):
+            def every(act):
+                def go():
+                    for piece in pieces:
+                        getattr(text_copy(piece, device, kind), act)()
+
+                if condition is None:
+                    go()
+                else:
+                    pl.when(condition)(go)
+
+            every("start")
+            pushed.append(every)
+
+        def chain_send(step):
+            low, high = layer - (step - 1), layer + (step - 1)
+            push(pair(low), me + 4, 2, (layer < outer - 1) & (low >= 0))
+            push(pair(high), me - 4, 3, (layer > 0) & (high < outer))
+
+        def chain_recv(step):
+            for at, there in ((layer - step, layer >= step), (layer + step, layer + step < outer)):
+
+                @pl.when(there)
+                def _():
+                    for piece in pair(at):
+                        text_copy(piece, mate, 1).wait_recv()
+
+                push(pair(at), mate, 1, there)
+
+        for load in loads[:2]:
+            load.wait()
+        push([me], cross, 0)
+        push([me], mate, 1)
 
     for side in range(2):
 
@@ -141,7 +172,7 @@
 
             lax.fori_loop(0, CHUNKS, step, 0)
 
-    for load in loads:
+    for load in loads[2 if inside else 0 : 4]:
         load.wait()
 
     def delta_step(h, carry):
@@ -153,8 +184,10 @@
         return carry
 
     lax.fori_loop(0, HEADS, delta_step, 0)
+    lane = lax.broadcasted_iota(jnp.int32, win_ref.shape, 1)
+    weights = jnp.sum(jnp.where(lane == me, win_ref[...], 0), axis=1, keepdims=True)
     for index, offset in enumerate((0, 2, 1)):
-        bias = jnp.where(win_ref[me, offset] > 0, 0.0, FAR).astype(jnp.float32)
+        bias = jnp.where(weights[offset : offset + 1] > 0, 0.0, FAR)
         stat[index, :HEADS, :] = sums_ref[...] + bias
     for side in range(2):
 
@@ -171,9 +204,11 @@
 
     if inside:
         text_copy(cross, cross, 0).wait_recv()
-        for peer in peers:
-            push(cross, peer)
-        push(cross, mate)
+        push([cross], mate, 1)
+        chain_send(1)
+
+    for load in loads[4:]:
+        load.wait()
 
     def own_step(h, carry):
         cols = head(h)
@@ -186,23 +221,27 @@
         dv_sum[:, cols] = dv
         return carry
 
-    lax.fori_loop(0, HEADS, own_step, 0)
+    if inside:
+        done = 0
+        for step in range(1, outer):
+            upto = HEADS * step // (outer - 1)
+            lax.fori_loop(done, upto, own_step, 0)
+            done = upto
+            chain_recv(step)
+            if step < outer - 1:
+                chain_send(step + 1)
+    else:
+        lax.fori_loop(0, HEADS, own_step, 0)
 
     line = lax.broadcasted_iota(jnp.int32, (TEXT, 1), 0)
     if inside:
-        for peer in peers:
-            for piece in (peer, peer + 2 - 4 * cross_bit):
-                text_copy(piece, mate, 0).wait_recv()
-                push(piece, mate)
-        for device in [me] + peers:
-            mates = device + 1 - 2 * core
-            for piece in (mates, mates + 2 - 4 * cross_bit):
-                text_copy(piece, mate, 0).wait_recv()
+        for at in range(outer):
+            piece = at * 4 + lax.rem(mate, 4)
+            for one in (piece, piece + 2 - 4 * cross_bit):
+                text_copy(one, mate, 1).wait_recv()
         spot = line // share
         place = (lax.rem(spot, half) * 2 + spot // half) * share + lax.rem(line, share)
     else:
-        text[0] = tk_ref[...]
-        text[1] = tv_ref[...]
         place = line
     valid = place < len_ref[0]
 
@@ -338,7 +377,9 @@
             stat_copy(side).wait_send()
 
     if inside:
-        for copy in text_copies + [copy1] + copies2 + [copy3]:
+        for every in pushed:
+            every("wait_send")
+        for copy in [copy1] + copies2 + [copy3]:
             copy.wait_send()
 
 
@@ -357,18 +398,18 @@
     text_out = jax.ShapeDtypeStruct(text_keys.shape, low if inside else wide)
     vmem, dma = pltpu.VMEM, pltpu.SemaphoreType.DMA
     scratch = [
-        vmem((tile, width), low), vmem((tile, width), low),
+        *[vmem((tile, width), low)] * 5,
         vmem((2, tile, width), low), vmem((2, tile, width), low),
         vmem((3, 2 * HEADS, tile), wide), vmem((2, 2 * HEADS, tile), wide),
         vmem((tile, width), wide), vmem((tile, width), wide), vmem((tile, width), wide),
         vmem((2, tile, width), low), vmem((2, tile, width), low),
         vmem((2, TEXT, width), low), vmem((2, TEXT, width), wide),
-        dma((2,)), dma((2, 2, CHUNKS)), dma((2, 2, CHUNKS)),
+        dma((7,)), dma((2, 2, CHUNKS)), dma((2, 2, CHUNKS)),
         dma((2,)), dma((2,)), dma((2, CHUNKS)), dma((2, CHUNKS)),
     ]
     if inside:
         scratch += [
-            dma((n - 1,)), dma((n,)),
+            dma((4, n)), dma((n,)),
             vmem((2, TEXT // 2, width), low), vmem((2, TEXT // 2, width), low),
             vmem((n // 4 - 1, 2, 2 * share, width), low), vmem((n // 4 - 1, 2, 2 * share, width), low),
             vmem((2, 2 * share, width), wide),
@@ -381,15 +422,15 @@
     dq, dk, dv, tdk, tdv = pl.pallas_call(
         functools.partial(kernel, n, inside),
         out_shape=(video_out, video_out, video_out, text_out, text_out),
-        in_specs=[hbm, hbm] + [on_chip] * 6 + [scalars] * 2,
+        in_specs=[hbm] * 5 + [on_chip, hbm, hbm, on_chip, scalars],
         out_specs=[on_chip] * 5,
         scratch_shapes=scratch,
         compiler_params=pltpu.CompilerParams(
-            collective_id=0, has_side_effects=True, vmem_limit_bytes=48 * 2**20
+            collective_id=0, has_side_effects=True, vmem_limit_bytes=62 * 2**20
         ),
     )(
         queries, out_grad, video_keys, video_values, attn_out, log_sums, text_keys, text_values,
-        window, text_len,
+        window.T, text_len,
     )
     if not inside:
         tdk = lax.psum_scatter(tdk, "seq", scatter_dimension=0, tiled=True).astype(low)

time: 88.7 us -> 87 us (0.981)
  the two profiles are of different devices: /device:TPU:19 before, /device:TPU:10 now
where the time goes in v2:
time: 87 us; the launch traced here: 86.7 us
  Pallas kernels  79.5 us (91%)
  local copies, waits for them, and re-layouts  5.87 us (7%)
  between operations  1.3 us (1%)
    pallas_call x1, Pallas kernels, local(): pl.pallas_call(functools.partial(kernel, n, inside), out_shape=(video_out...  79.5 us
    unnamed x13, local copies, waits for them, and re-layouts  5.87 us

profile of v2, /device:TPU:10, one launch (start us, length us, event | category | flops | bytes accessed | tf_op | source)
XLA Modules:
  0.0 86.7 jit_solution(8329310827885707216)
XLA Ops:
  1.3 79.5 %shard_map.137 = (bf16[256,1536]{1,0:T(8,128)(2,1)}, bf16[256,1536]{1,0:T(8,128)(2,1)}, bf16[256,1536]{1,0:T(8,128)(2,1)}, bf16[16,1536]{1,0:T(8,128)(2,1)}, bf16[16,1536]{1,0:T(8,128)(2,1)}) custom-call(bf16[256,1536]{1,0:T(8,128)(2,1)} %q_any.1, bf16[256,1536]{1,0:T(8,128)(2,1)} %g_any.1, bf16[256,1536]{1,0:T(8,128)(2,1)} %k_any.1, ...), custom_call_target="tpu_custom_call" | custom-call | tf_op jit(solution)/shard_map/pallas_call | solution.py:422
  80.8 0.0 copy-start.1
  80.8 2.1 %copy.21 = bf16[256,1536]{1,0:T(8,128)(2,1)} copy(bf16[256,1536]{1,0:T(8,128)(2,1)} %get-tuple-element.10) | data formatting | bytes 1572864
  83.0 0.0 copy-done.1
  83.0 0.0 copy-start
  83.0 0.9 %copy.22 = bf16[256,1536]{1,0:T(8,128)(2,1)} copy(bf16[256,1536]{1,0:T(8,128)(2,1)S(1)} %copy-done.1) | data formatting | bytes 1572864
  83.9 0.5 copy-done
  84.4 0.0 copy-start.3
  84.4 0.9 %copy.23 = bf16[256,1536]{1,0:T(8,128)(2,1)} copy(bf16[256,1536]{1,0:T(8,128)(2,1)S(1)} %copy-done) | data formatting | bytes 1572864
  85.3 0.0 copy-done.3
  85.3 0.0 copy-start.2
  85.3 0.6 copy.24
  85.9 0.2 copy-done.2
  86.1 0.6 copy.25
Async XLA Ops:
  80.8 2.1 %copy-start.1 = (bf16[256,1536]{1,0:T(8,128)(2,1)S(1)}, bf16[256,1536]{1,0:T(8,128)(2,1)}, u32[]{:S(2)}) copy-start(bf16[256,1536]{1,0:T(8,128)(2,1)} %get-tuple-element.11) | copy-start | bytes 2359300
  83.0 1.4 %copy-start = (bf16[256,1536]{1,0:T(8,128)(2,1)S(1)}, bf16[256,1536]{1,0:T(8,128)(2,1)}, u32[]{:S(2)}) copy-start(bf16[256,1536]{1,0:T(8,128)(2,1)} %get-tuple-element.12) | copy-start | bytes 2359300
  84.4 0.9 %copy-start.3 = (bf16[16,1536]{1,0:T(8,128)(2,1)S(1)}, bf16[16,1536]{1,0:T(8,128)(2,1)}, u32[]{:S(2)}) copy-start(bf16[16,1536]{1,0:T(8,128)(2,1)} %get-tuple-element.13) | copy-start | bytes 147460
  85.3 0.8 copy-start.2

commit v3 on v2

v3 whole, which is shorter than its diff:
```python
import functools

import jax
import jax.numpy as jnp
from jax import lax
from jax.experimental import pallas as pl
from jax.experimental.pallas import tpu as pltpu
from jax.sharding import PartitionSpec as P

HEADS = 12
HEAD_DIM = 128
TEXT = 256
GROUP = 2
CHUNKS = HEADS // GROUP
FACTOR = HEAD_DIM ** (-0.5)
FAR = 1e30
PACE = (0, 1, 2, 3, 4, 5, 6)
SPLIT = (1, 3, 5)
MESH = pl.DeviceIdType.MESH


def mm(a, b, ca, cb):
    return lax.dot_general(a, b, (((ca,), (cb,)), ((), ())), preferred_element_type=jnp.float32)


def block_grads(q, g, k, v, sums, deltas, valid=None):
    probs = jnp.exp(mm(k, q, 1, 1) * FACTOR - sums)
    if valid is not None:
        probs = jnp.where(valid, probs, 0.0)
    dprobs = mm(v, g, 1, 1)
    dscores = (probs * (dprobs - deltas)).astype(jnp.bfloat16)
    dq = mm(dscores, k, 0, 0) * FACTOR
    dk = mm(dscores, q, 1, 0) * FACTOR
    dv = mm(probs.astype(jnp.bfloat16), g, 1, 0)
    return dq, dk, dv


def head(h):
    return pl.ds(pl.multiple_of(h * HEAD_DIM, HEAD_DIM), HEAD_DIM)


def kernel(
    n, inside, q_any, g_any, k_any, v_any, o_any, sums_ref, tk_any, tv_any, win_ref, len_ref,
    dq_ref, dk_ref, dv_ref, tdk_ref, tdv_ref,
    q_ref, g_ref, k_ref, v_ref, o_ref, nq, ng, stat, nstat, dq_sum, dk_sum, dv_sum, dq_out, dq_in, text, tgrad,
    local_sem, in_send, in_recv, stat_send, stat_recv, dq_send, dq_recv,
    *more,
):
    me = lax.axis_index("seq")
    share = TEXT // n
    half, outer = n // 2, n // 4
    core, cross_bit, layer = lax.rem(me, 2), lax.rem(me // 2, 2), me // 4
    mate, cross = me + 1 - 2 * core, me + 2 - 4 * cross_bit
    close, wide = 1 - core, core
    far = me - 1 + 2 * wide
    has_far = (far >= 0) & (far < n)
    corner = core == cross_bit
    odd, high = lax.rem(layer, 2), lax.rem(layer // 2, 2)
    next_layer, leap_layer = layer + 1 - 2 * odd, layer + 2 - 4 * high
    step_on, leap = next_layer * 4 + lax.rem(me, 4), leap_layer * 4 + lax.rem(me, 4)
    peers = [step_on, leap]

    own_text = pl.ds(pl.multiple_of((core * half + me // 2) * share, share), share)
    loads = [
        pltpu.make_async_copy(src, dst, local_sem.at[i])
        for i, (src, dst) in enumerate((
            (tk_any, text.at[0, own_text, :] if inside else text.at[0]),
            (tv_any, text.at[1, own_text, :] if inside else text.at[1]),
            (g_any, g_ref), (o_any, o_ref), (q_any, q_ref), (k_any, k_ref), (v_any, v_ref),
        ))
    ]
    for load in loads:
        load.start()

    def signal(device):
        pl.semaphore_signal(barrier, inc=1, device_id={"seq": device}, device_id_type=MESH)

    def remote(src, dst, send, recv, device):
        return pltpu.make_async_remote_copy(
            src_ref=src, dst_ref=dst, send_sem=send, recv_sem=recv,
            device_id={"seq": device}, device_id_type=MESH,
        )

    barrier = pltpu.get_barrier_semaphore()
    known = [mate] + ([cross] + peers if inside else [])
    for device in known:
        signal(device)
    pl.when(has_far)(functools.partial(signal, far))
    pl.semaphore_wait(barrier, len(known) + has_far.astype(jnp.int32))

    def near(side):
        return me - 1 + 2 * side

    def far_only(go):
        pl.when(has_far)(go)

    def always(go):
        go()

    def columns(c):
        return pl.ds(pl.multiple_of(c * GROUP * HEAD_DIM, GROUP * HEAD_DIM), GROUP * HEAD_DIM)

    def in_copies(side, c):
        there = 1 - side
        return [
            remote(
                src.at[:, columns(c)], dst.at[there, :, columns(c)],
                in_send.at[i, there, c], in_recv.at[i, there, c], near(side),
            )
            for i, (src, dst) in enumerate(((q_any, nq), (g_any, ng)))
        ]

    def stat_copy(side):
        there = 1 - side
        return remote(
            stat.at[side], nstat.at[there], stat_send.at[there], stat_recv.at[there], near(side)
        )

    def dq_copy(side, c):
        there = 1 - side
        return remote(
            dq_out.at[side, :, columns(c)], dq_in.at[there, :, columns(c)],
            dq_send.at[there, c], dq_recv.at[there, c], near(side),
        )

    if inside:
        t_send, t_recv, part1, got1, part2, got2, sum3, part3, got3, r1, r2, r3 = more

        def slot(device):
            return lax.rem(device, 2) * half + device // 2

        def rows(device):
            return pl.ds(pl.multiple_of(slot(device) * share, share), share)

        def text_copy(piece, device, kind):
            ref = text.at[:, rows(piece), :]
            return remote(ref, ref, t_send.at[kind, piece], t_recv.at[piece], device)

        def pair(at):
            own = at * 4 + lax.rem(me, 4)
            return own, own + 2 - 4 * cross_bit

        def arrive(*pieces):
            for piece in pieces:
                text_copy(piece, mate, 1).wait_recv()

        pushed = []

        def push(device, kind, *pieces):
            for piece in pieces:
                copy = text_copy(piece, device, kind)
                copy.start()
                pushed.append(copy)

        for load in loads[:2]:
            load.wait()
        push(cross, 0, me)
        push(leap, 2, me)
        push(step_on, 3, me)
        push(mate, 1, me)

    def send_in(side, first=0, end=CHUNKS):
        def step(c, carry):
            for copy in in_copies(side, c):
                copy.start()
            return carry

        lax.fori_loop(first, end, step, 0)

    def send_far(stage):
        first, end = PACE[stage], PACE[stage + 1]
        if first < end:
            far_only(functools.partial(send_in, wide, first, end))

    send_in(close)
    send_far(0)

    for load in loads[2 if inside else 0 : 4]:
        load.wait()

    def delta_step(h, carry):
        cols = head(h)
        prod = g_ref[:, cols].astype(jnp.float32) * o_ref[:, cols].astype(jnp.float32)
        row = jnp.sum(prod.T, axis=0, keepdims=True)
        for side in range(3):
            stat[side, pl.ds(HEADS + h, 1), :] = row
        return carry

    lax.fori_loop(0, HEADS, delta_step, 0)
    lane = lax.broadcasted_iota(jnp.int32, win_ref.shape, 1)
    weights = jnp.sum(jnp.where(lane == me, win_ref[...], 0), axis=1, keepdims=True)
    for index, offset in enumerate((0, 2, 1)):
        bias = jnp.where(weights[offset : offset + 1] > 0, 0.0, FAR)
        stat[index, :HEADS, :] = sums_ref[...] + bias
    stat_copy(close).start()
    far_only(lambda: stat_copy(wide).start())

    @pl.when(jnp.logical_not(has_far))
    def _():
        nq[wide] = jnp.zeros(nq.shape[1:], nq.dtype)
        ng[wide] = jnp.zeros(ng.shape[1:], ng.dtype)
        dq_in[wide] = jnp.zeros(dq_in.shape[1:], dq_in.dtype)
        nstat[wide] = jnp.full(nstat.shape[1:], FAR, nstat.dtype)

    if inside:
        arrive(cross)
        push(leap, 2, cross)
        push(step_on, 3, cross)
        push(mate, 1, cross)

    for load in loads[4:]:
        load.wait()

    def own_step(h, carry):
        cols = head(h)
        dq, dk, dv = block_grads(
            q_ref[:, cols], g_ref[:, cols], k_ref[:, cols], v_ref[:, cols],
            stat[2, pl.ds(h, 1), :], stat[2, pl.ds(HEADS + h, 1), :],
        )
        dq_sum[:, cols] = dq
        dk_sum[:, cols] = dk
        dv_sum[:, cols] = dv
        return carry

    lax.fori_loop(0, HEADS // 2, own_step, 0)
    send_far(1)
    lax.fori_loop(HEADS // 2, HEADS, own_step, 0)
    send_far(2)
    if inside:
        arrive(*pair(leap_layer))
        push(step_on, 3, *pair(leap_layer))
        push(mate, 1, *pair(leap_layer))

    def window_step(side, where, last, c, carry):
        @where
        def _():
            for copy in in_copies(1 - side, c):
                copy.wait_recv()

        for i in range(GROUP):
            h = c * GROUP + i
            cols = head(h)
            dq, dk, dv = block_grads(
                nq[side, :, cols], ng[side, :, cols], k_ref[:, cols], v_ref[:, cols],
                nstat[side, pl.ds(h, 1), :], nstat[side, pl.ds(HEADS + h, 1), :],
            )
            dq_out[side, :, cols] = dq.astype(jnp.bfloat16)
            if last:
                dk_ref[:, cols] = (dk_sum[:, cols] + dk).astype(jnp.bfloat16)
                dv_ref[:, cols] = (dv_sum[:, cols] + dv).astype(jnp.bfloat16)
            else:
                dk_sum[:, cols] += dk
                dv_sum[:, cols] += dv

        @where
        def _():
            dq_copy(side, c).start()

        return carry

    mate_step = functools.partial(window_step, close, always, False)
    far_step = functools.partial(window_step, wide, far_only, True)
    stat_copy(1 - close).wait_recv()
    lax.fori_loop(0, CHUNKS // 2, mate_step, 0)
    if inside:
        for at in (next_layer, next_layer + 2 - 4 * high):
            arrive(*pair(at))
            push(mate, 1, *pair(at))
    send_far(3)
    lax.fori_loop(CHUNKS // 2, CHUNKS, mate_step, 0)
    send_far(4)
    far_only(lambda: stat_copy(1 - wide).wait_recv())

    line = lax.broadcasted_iota(jnp.int32, (TEXT, 1), 0)
    if inside:
        for at in range(outer):
            piece = at * 4 + lax.rem(mate, 4)
            arrive(piece, piece + 2 - 4 * cross_bit)
        spot = line // share
        place = (lax.rem(spot, half) * 2 + spot // half) * share + lax.rem(line, share)
    else:
        place = line
    valid = place < len_ref[0]

    def text_step(h, carry):
        cols = head(h)
        dq, dk, dv = block_grads(
            q_ref[:, cols], g_ref[:, cols], text[0, :, cols], text[1, :, cols],
            sums_ref[pl.ds(h, 1), :], stat[2, pl.ds(HEADS + h, 1), :], valid,
        )
        dq_sum[:, cols] += dq
        tgrad[0, :, cols] = dk
        tgrad[1, :, cols] = dv
        return carry

    lax.fori_loop(0, HEADS // 2, text_step, 0)
    send_far(5)
    lax.fori_loop(HEADS // 2, HEADS, text_step, 0)

    if inside:
        rest = half * share
        pair_rows = 2 * share

        def span(start, size):
            return pl.ds(pl.multiple_of(start, share), size)

        part1[...] = tgrad[:, span((1 - core) * rest, rest), :].astype(jnp.bfloat16)
        copy1 = remote(part1, got1, r1.at[0], r1.at[1], mate)
        copy1.start()

    lax.fori_loop(0, SPLIT[0], far_step, 0)

    if inside:
        copy1.wait_recv()
        def kept(at):
            return tgrad[:, span(core * rest + at * pair_rows, pair_rows), :] + got1[
                :, span(at * pair_rows, pair_rows), :
            ].astype(jnp.float32)

        for i in range(2):
            part2[i] = kept(1 - odd + 2 * i).astype(jnp.bfloat16)
        copy2 = remote(part2.at[:2], got2.at[:2], r2.at[0, 0], r2.at[1, 0], step_on)
        copy2.start()

    lax.fori_loop(SPLIT[0], SPLIT[1], far_step, 0)

    if inside:
        copy2.wait_recv()
        part2[2] = (kept(leap_layer) + got2[1 - high].astype(jnp.float32)).astype(jnp.bfloat16)
        copy4 = remote(part2.at[2], got2.at[2], r2.at[0, 1], r2.at[1, 1], leap)
        copy4.start()

    lax.fori_loop(SPLIT[1], SPLIT[2], far_step, 0)

    if inside:
        copy4.wait_recv()
        total = kept(layer) + got2[high].astype(jnp.float32) + got2[2].astype(jnp.float32)
        sum3[...] = total
        part3[...] = sum3[:, span((1 - cross_bit) * share, share), :].astype(jnp.bfloat16)
        copy3 = remote(part3, got3, r3.at[0], r3.at[1], cross)
        copy3.start()

    lax.fori_loop(SPLIT[2], CHUNKS, far_step, 0)

    if inside:
        copy3.wait_recv()
        mine = sum3[:, span(cross_bit * share, share), :] + got3[...].astype(jnp.float32)
        tdk_ref[...] = mine[0].astype(jnp.bfloat16)
        tdv_ref[...] = mine[1].astype(jnp.bfloat16)
    else:
        tdk_ref[...] = tgrad[0]
        tdv_ref[...] = tgrad[1]

    def last_step(c, carry):
        dq_copy(1 - close, c).wait_recv()
        far_only(lambda: dq_copy(1 - wide, c).wait_recv())
        cols = columns(c)
        dq_ref[:, cols] = (
            dq_sum[:, cols]
            + dq_in[0, :, cols].astype(jnp.float32)
            + dq_in[1, :, cols].astype(jnp.float32)
        ).astype(jnp.bfloat16)
        return carry

    lax.fori_loop(0, CHUNKS, last_step, 0)

    def finish(side):
        def step(c, carry):
            for copy in in_copies(side, c):
                copy.wait_send()
            dq_copy(side, c).wait_send()
            return carry

        lax.fori_loop(0, CHUNKS, step, 0)
        stat_copy(side).wait_send()

    finish(close)
    far_only(functools.partial(finish, wide))

    if inside:
        for copy in pushed + [copy1, copy2, copy4, copy3]:
            copy.wait_send()


def local(
    queries, video_keys, video_values, attn_out, out_grad, log_sums, text_keys, text_values,
    window, text_len,
):
    n = lax.axis_size("seq")
    tile, width = queries.shape
    share = TEXT // n
    inside = n == 16 and share % 16 == 0
    low, wide = jnp.bfloat16, jnp.float32
    if not inside:
        text_keys = lax.all_gather(text_keys, "seq", axis=0, tiled=True)
        text_values = lax.all_gather(text_values, "seq", axis=0, tiled=True)
    text_out = jax.ShapeDtypeStruct(text_keys.shape, low if inside else wide)
    vmem, dma = pltpu.VMEM, pltpu.SemaphoreType.DMA
    scratch = [
        *[vmem((tile, width), low)] * 5,
        vmem((2, tile, width), low), vmem((2, tile, width), low),
        vmem((3, 2 * HEADS, tile), wide), vmem((2, 2 * HEADS, tile), wide),
        vmem((tile, width), wide), vmem((tile, width), wide), vmem((tile, width), wide),
        vmem((2, tile, width), low), vmem((2, tile, width), low),
        vmem((2, TEXT, width), low), vmem((2, TEXT, width), wide),
        dma((7,)), dma((2, 2, CHUNKS)), dma((2, 2, CHUNKS)),
        dma((2,)), dma((2,)), dma((2, CHUNKS)), dma((2, CHUNKS)),
    ]
    if inside:
        scratch += [
            dma((4, n)), dma((n,)),
            vmem((2, TEXT // 2, width), low), vmem((2, TEXT // 2, width), low),
            vmem((3, 2, 2 * share, width), low), vmem((3, 2, 2 * share, width), low),
            vmem((2, 2 * share, width), wide),
            vmem((2, share, width), low), vmem((2, share, width), low),
            dma((2,)), dma((2, 2)), dma((2,)),
        ]
    hbm, on_chip = pl.BlockSpec(memory_space=pl.ANY), pl.BlockSpec(memory_space=pltpu.VMEM)
    scalars = pl.BlockSpec(memory_space=pltpu.SMEM)
    video_out = jax.ShapeDtypeStruct((tile, width), low)
    dq, dk, dv, tdk, tdv = pl.pallas_call(
        functools.partial(kernel, n, inside),
        out_shape=(video_out, video_out, video_out, text_out, text_out),
        in_specs=[hbm] * 5 + [on_chip, hbm, hbm, on_chip, scalars],
        out_specs=[on_chip] * 5,
        scratch_shapes=scratch,
        compiler_params=pltpu.CompilerParams(
            collective_id=0, has_side_effects=True, vmem_limit_bytes=62 * 2**20
        ),
    )(
        queries, out_grad, video_keys, video_values, attn_out, log_sums, text_keys, text_values,
        window.T, text_len,
    )
    if not inside:
        tdk = lax.psum_scatter(tdk, "seq", scatter_dimension=0, tiled=True).astype(low)
        tdv = lax.psum_scatter(tdv, "seq", scatter_dimension=0, tiled=True).astype(low)
    return dq, dk, dv, tdk, tdv


def solution(mesh):
    rows, every = P(("grp", "seq"), None), P()
    return jax.shard_map(
        local,
        mesh=mesh,
        in_specs=(rows, rows, rows, rows, rows, P(None, ("grp", "seq")), rows, rows, every, P("grp")),
        out_specs=(rows, rows, rows, rows, rows),
        check_vma=False,
    )
```

time: 87 us -> 74.4 us (0.86)
  the two profiles are of different devices: /device:TPU:10 before, /device:TPU:1 now
where the time goes in v3:
time: 74.4 us; the launch traced here: 74.1 us
  Pallas kernels  66.9 us (90%)
  local copies, waits for them, and re-layouts  5.87 us (8%)
  between operations  1.3 us (2%)
    pallas_call x1, Pallas kernels, local(): pl.pallas_call(functools.partial(kernel, n, inside), out_shape=(video_out...  66.9 us
    unnamed x13, local copies, waits for them, and re-layouts  5.87 us

profile of v3, /device:TPU:1, one launch (start us, length us, event | category | flops | bytes accessed | tf_op | source)
XLA Modules:
  0.0 74.1 jit_solution(8399693074643300474)
XLA Ops:
  1.3 66.9 %shard_map.137 = (bf16[256,1536]{1,0:T(8,128)(2,1)}, bf16[256,1536]{1,0:T(8,128)(2,1)}, bf16[256,1536]{1,0:T(8,128)(2,1)}, bf16[16,1536]{1,0:T(8,128)(2,1)}, bf16[16,1536]{1,0:T(8,128)(2,1)}) custom-call(bf16[256,1536]{1,0:T(8,128)(2,1)} %q_any.1, bf16[256,1536]{1,0:T(8,128)(2,1)} %g_any.1, bf16[256,1536]{1,0:T(8,128)(2,1)} %k_any.1, ...), custom_call_target="tpu_custom_call" | custom-call | tf_op jit(solution)/shard_map/pallas_call | solution.py:421
  68.2 0.0 copy-start.1
  68.2 2.1 %copy.21 = bf16[256,1536]{1,0:T(8,128)(2,1)} copy(bf16[256,1536]{1,0:T(8,128)(2,1)} %get-tuple-element.10) | data formatting | bytes 1572864
  70.3 0.0 copy-done.1
  70.3 0.0 copy-start
  70.3 0.9 %copy.22 = bf16[256,1536]{1,0:T(8,128)(2,1)} copy(bf16[256,1536]{1,0:T(8,128)(2,1)S(1)} %copy-done.1) | data formatting | bytes 1572864
  71.2 0.5 copy-done
  71.7 0.0 copy-start.3
  71.7 0.9 %copy.23 = bf16[256,1536]{1,0:T(8,128)(2,1)} copy(bf16[256,1536]{1,0:T(8,128)(2,1)S(1)} %copy-done) | data formatting | bytes 1572864
  72.6 0.0 copy-done.3
  72.6 0.0 copy-start.2
  72.6 0.6 copy.24
  73.2 0.2 copy-done.2
  73.4 0.6 copy.25
Async XLA Ops:
  68.2 2.1 %copy-start.1 = (bf16[256,1536]{1,0:T(8,128)(2,1)S(1)}, bf16[256,1536]{1,0:T(8,128)(2,1)}, u32[]{:S(2)}) copy-start(bf16[256,1536]{1,0:T(8,128)(2,1)} %get-tuple-element.11) | copy-start | bytes 2359300
  70.3 1.4 %copy-start = (bf16[256,1536]{1,0:T(8,128)(2,1)S(1)}, bf16[256,1536]{1,0:T(8,128)(2,1)}, u32[]{:S(2)}) copy-start(bf16[256,1536]{1,0:T(8,128)(2,1)} %get-tuple-element.12) | copy-start | bytes 2359300
  71.7 0.9 %copy-start.3 = (bf16[16,1536]{1,0:T(8,128)(2,1)S(1)}, bf16[16,1536]{1,0:T(8,128)(2,1)}, u32[]{:S(2)}) copy-start(bf16[16,1536]{1,0:T(8,128)(2,1)} %get-tuple-element.13) | copy-start | bytes 147460
  72.6 0.8 %copy-start.2 = (bf16[16,1536]{1,0:T(8,128)(2,1)S(1)}, bf16[16,1536]{1,0:T(8,128)(2,1)}, u32[]{:S(2)}) copy-start(bf16[16,1536]{1,0:T(8,128)(2,1)} %get-tuple-element.14) | copy-start | bytes 147460

commit v4 on v3

--- a/solution.py
+++ b/solution.py
@@ -15,7 +15,8 @@
 FACTOR = HEAD_DIM ** (-0.5)
 FAR = 1e30
 PACE = (0, 1, 2, 3, 4, 5, 6)
-SPLIT = (1, 3, 5)
+EARLY = (1, 2)
+SPLIT = (2, 4, 5)
 MESH = pl.DeviceIdType.MESH
 
 
@@ -262,6 +263,8 @@
     far_step = functools.partial(window_step, wide, far_only, True)
     stat_copy(1 - close).wait_recv()
     lax.fori_loop(0, CHUNKS // 2, mate_step, 0)
+    far_only(lambda: stat_copy(1 - wide).wait_recv())
+    lax.fori_loop(0, EARLY[0], far_step, 0)
     if inside:
         for at in (next_layer, next_layer + 2 - 4 * high):
             arrive(*pair(at))
@@ -269,7 +272,7 @@
     send_far(3)
     lax.fori_loop(CHUNKS // 2, CHUNKS, mate_step, 0)
     send_far(4)
-    far_only(lambda: stat_copy(1 - wide).wait_recv())
+    lax.fori_loop(EARLY[0], EARLY[1], far_step, 0)
 
     line = lax.broadcasted_iota(jnp.int32, (TEXT, 1), 0)
     if inside:
@@ -308,7 +311,7 @@
         copy1 = remote(part1, got1, r1.at[0], r1.at[1], mate)
         copy1.start()
 
-    lax.fori_loop(0, SPLIT[0], far_step, 0)
+    lax.fori_loop(EARLY[1], SPLIT[0], far_step, 0)
 
     if inside:
         copy1.wait_recv()
@@ -380,6 +383,19 @@
     if inside:
         for copy in pushed + [copy1, copy2, copy4, copy3]:
             copy.wait_send()
+
+
+def hand_over(*refs):
+    inputs, outputs, held, sem = refs[:5], refs[5:10], refs[10:15], refs[15]
+    loads = [pltpu.make_async_copy(inputs[i], held[i], sem.at[0, i]) for i in range(5)]
+    stores = [pltpu.make_async_copy(held[i], outputs[i], sem.at[1, i]) for i in range(5)]
+    for load in loads:
+        load.start()
+    for load, store in zip(loads, stores):
+        load.wait()
+        store.start()
+    for store in stores:
+        store.wait()
 
 
 def local(
@@ -418,7 +434,7 @@
     hbm, on_chip = pl.BlockSpec(memory_space=pl.ANY), pl.BlockSpec(memory_space=pltpu.VMEM)
     scalars = pl.BlockSpec(memory_space=pltpu.SMEM)
     video_out = jax.ShapeDtypeStruct((tile, width), low)
-    dq, dk, dv, tdk, tdv = pl.pallas_call(
+    results = pl.pallas_call(
         functools.partial(kernel, n, inside),
         out_shape=(video_out, video_out, video_out, text_out, text_out),
         in_specs=[hbm] * 5 + [on_chip, hbm, hbm, on_chip, scalars],
@@ -431,6 +447,15 @@
         queries, out_grad, video_keys, video_values, attn_out, log_sums, text_keys, text_values,
         window.T, text_len,
     )
+    shapes = [video_out] * 3 + [text_out] * 2
+    dq, dk, dv, tdk, tdv = pl.pallas_call(
+        hand_over,
+        out_shape=shapes,
+        in_specs=[hbm] * 5,
+        out_specs=[hbm] * 5,
+        scratch_shapes=[vmem(one.shape, one.dtype) for one in shapes] + [dma((2, 5))],
+        compiler_params=pltpu.CompilerParams(vmem_limit_bytes=62 * 2**20),
+    )(*results)
     if not inside:
         tdk = lax.psum_scatter(tdk, "seq", scatter_dimension=0, tiled=True).astype(low)
         tdv = lax.psum_scatter(tdv, "seq", scatter_dimension=0, tiled=True).astype(low)

time: 74.4 us -> 70 us (0.941)
  local copies, waits for them, and re-layouts: 5.87 us -> 0 us
  Pallas kernels: 66.9 us -> 68.4 us
    unnamed x13 -> x0, local copies, waits for them, and re-layouts: 5.87 us -> none
    pallas_call x0 -> x1, Pallas kernels: none -> 2.63 us  [local(): pl.pallas_call(hand_over, out_shape=shapes, in_specs=[hbm] * 5, out_specs...]
    pallas_call x1, Pallas kernels: 66.9 us -> 65.8 us  [local(): pl.pallas_call(functools.partial(kernel, n, inside), out_shape=(video_out...]
where the time goes in v4:
time: 70 us; the launch traced here: 69.7 us
  Pallas kernels  68.4 us (98%)
  between operations  1.29 us (2%)
    pallas_call x1, Pallas kernels, local(): pl.pallas_call(functools.partial(kernel, n, inside), out_shape=(video_out...  65.8 us
    pallas_call x1, Pallas kernels, local(): pl.pallas_call(hand_over, out_shape=shapes, in_specs=[hbm] * 5, out_specs...  2.63 us

profile of v4, /device:TPU:1, one launch (start us, length us, event | category | flops | bytes accessed | tf_op | source)
XLA Modules:
  0.0 69.7 jit_solution(13407132515796128006)
XLA Ops:
  1.3 65.8 %shard_map.137 = (bf16[256,1536]{1,0:T(8,128)(2,1)}, bf16[256,1536]{1,0:T(8,128)(2,1)}, bf16[256,1536]{1,0:T(8,128)(2,1)}, bf16[16,1536]{1,0:T(8,128)(2,1)}, bf16[16,1536]{1,0:T(8,128)(2,1)}) custom-call(bf16[256,1536]{1,0:T(8,128)(2,1)} %q_any.1, bf16[256,1536]{1,0:T(8,128)(2,1)} %g_any.1, bf16[256,1536]{1,0:T(8,128)(2,1)} %k_any.1, ...), custom_call_target="tpu_custom_call" | custom-call | tf_op jit(solution)/shard_map/pallas_call | solution.py:437
  67.1 2.6 %shard_map.138 = (bf16[256,1536]{1,0:T(8,128)(2,1)}, bf16[256,1536]{1,0:T(8,128)(2,1)}, bf16[256,1536]{1,0:T(8,128)(2,1)}, bf16[16,1536]{1,0:T(8,128)(2,1)}, bf16[16,1536]{1,0:T(8,128)(2,1)}) custom-call(bf16[256,1536]{1,0:T(8,128)(2,1)} %get-tuple-element.10.refs_0_, bf16[256,1536]{1,0:T(8,128)(2,1)} %get-tuple-element.11.refs_1_, ...), custom_call_target="tpu_custom_call" | custom-call | tf_op jit(solution)/shard_map/pallas_call | solution.py:451
